TPU v7x, 32 devices: a whole 2x2x4 slice. The times are simulated.
32 devices in a mesh: row: 8 (over z, core), col: 4 (over y, x).
Axes of the slice: x: 2, y: 2, z: 4, core: 2. Of those that a mesh axis runs over, the one named last changes fastest.
Arguments:
- occ_irrep: int32 [128], replicated, may hold values from 0 to 7
- vir_irrep: int32 [1024], replicated, may hold values from 0 to 7
- w_slab: bfloat16 [3072, 131072], P('row', 'col'), may hold values from -0.046875 to 0.046875
- amplitudes: bfloat16 [256, 131072], P('row', 'col'), may hold values from -6 to 6
Outputs:
- cycle_term: float32 [256, 3072], P('col', 'row')
Inputs may be any that keep to these rules, and one draw needn't show every extreme that they name: `occ_irrep`: D2h irrep labels. `vir_irrep`: D2h irrep labels.
All inputs are finite; a program needn't handle non-finite values.
Results may differ from a plain program's by a relative error of at most 0.0003.
Values may be sent and summed in bfloat16 or wider, within the bound.
A program may use at most 128 MiB of HBM per device.

v0:
```python
import jax
import jax.numpy as jnp
from jax import lax
from jax.sharding import PartitionSpec as P


def labels(index, occ_irrep, vir_irrep):
    nvir = vir_irrep.shape[0]
    occ_part = jnp.take(occ_irrep, index // nvir)
    vir_part = jnp.take(vir_irrep, index % nvir)
    return jnp.bitwise_xor(occ_part, vir_part)


def body(occ_irrep, vir_irrep, w_slab, amplitudes):
    nrows, width = w_slab.shape
    row_start = lax.axis_index("row") * nrows
    col_start = lax.axis_index("col") * width
    row_labels = labels(row_start + jnp.arange(nrows, dtype=jnp.int32), occ_irrep, vir_irrep)
    col_labels = labels(col_start + jnp.arange(width, dtype=jnp.int32), occ_irrep, vir_irrep)
    keep = row_labels[:, None] == col_labels[None, :]
    masked = jnp.where(keep, w_slab, jnp.zeros_like(w_slab))
    dims = (((1,), (1,)), ((), ()))
    gathered = lax.all_gather(amplitudes, "row", axis=0, tiled=True)
    return lax.psum_scatter(
        lax.dot_general(gathered, masked, dims, preferred_element_type=jnp.float32),
        "col",
        scatter_dimension=0,
        tiled=True,
    )


def solution(mesh):
    placed = (P(), P(), P("row", "col"), P("row", "col"))
    return jax.shard_map(
        body, mesh=mesh, in_specs=placed, out_specs=P("col", "row"), check_vma=False
    )
```

profile of v0, /device:TPU:6, one launch (start us, length us, event | category | flops | bytes accessed | tf_op | source)
XLA Modules:
  0.0 385.7 jit_solution(7259818871316264346)
XLA Ops:
  6.5 0.0 copy-start
  6.5 0.0 all-gather.2.cloned.1.call-start
  6.5 0.7 all-gather.2.cloned.1.call-update
  7.3 0.0 reduce-scatter.4.cloned.1.call-start
  7.4 0.0 copy-done
  7.4 1.9 gather_fusion.1
  9.3 1.2 compare_select_fusion.4
  10.5 0.0 copy-start.1
  10.5 130.0 %gather_fusion.3 = s32[32768]{0:T(1024)S(1)} fusion(s32[1024]{0:T(1024)S(1)} %copy-done, s32[32768]{0:T(1024)S(1)} %broadcast_clamp_fusion), kind=kCustom, calls=%fused_computation.3 | custom fusion | bytes 393216 | tf_op jit(solution)/shard_map/jit(_take)/gather | solution.py:10
  140.5 0.0 copy-done.1
  140.5 2.7 gather_fusion
  143.3 193.9 %gather_fusion.2 = s32[32768]{0:T(1024)S(1)} fusion(s32[128]{0:T(128)S(1)} %copy-done.1, s32[32768]{0:T(1024)S(1)} %broadcast_clamp_fusion.1), kind=kCustom, calls=%fused_computation.2 | custom fusion | bytes 393216 | tf_op jit(solution)/shard_map/jit(_take)/gather | solution.py:9
  337.2 0.2 select_xor_fusion
  337.4 0.0 all-gather.2.cloned.1.call-done
  337.4 15.7 %fusion.4 = f32[256,384]{0,1:T(8,128)S(1)} fusion(bf16[256,32768]{1,0:T(8,128)(2,1)} %all-gather.2.cloned.1.call-done, bf16[384,32768]{1,0:T(8,128)(2,1)} %param.6, s32[32768]{0:T(1024)S(1)} %select_xor_fusion, s32[384]{0:T(512)S(1)} %select_xor_fusion.1), kind=kOutput, calls=%fused_computation.9 | convolution fusion | flops 6467616768 | bytes 42468864 | tf_op jit(solution)/shard_map/dot_general | solution.py:25
  353.1 0.9 copy.8
  354.0 0.0 reduce-scatter.4.cloned.1.call-update
  354.0 24.8 %reduce-scatter.4.cloned.1.call-done = f32[64,384]{1,0:T(8,128)} async-done(((f32[256,384]{1,0:T(8,128)}), f32[64,384]{1,0:T(8,128)}) %reduce-scatter.4.cloned.1.call-update) | async-done | bytes 98320 | tf_op jit(solution)/shard_map/reduce_scatter | solution.py:24
  (6 shorter events, 0.1 us)
Async XLA Ops:
  6.5 0.8 copy-start
  6.5 330.9 %all-gather.2.cloned.1.call-start = ((), (), s32[]{:S(2)}) async-start(), calls=%async_computation.1 | async-start | bytes 18874368 | tf_op jit(solution)/shard_map/all_gather | solution.py:23
  7.3 371.6 %reduce-scatter.4.cloned.1.call-start = ((), (), s32[]{:S(2)}) async-start(), calls=%async_computation.2 | async-start | bytes 491520 | tf_op jit(solution)/shard_map/reduce_scatter | solution.py:24
  10.5 130.1 %copy-start.1 = (s32[128]{0:T(128)S(1)}, s32[128]{0:T(128)}, u32[]{:S(2)}) copy-start(s32[128]{0:T(128)} %param.4) | copy-start | bytes 1540
Sparse Core Ops, SparseCore 0:
  9.0 152.2 all-gather.1
  354.2 24.6 reduce-scatter.3
where the time goes:
time: 388 us; the launch traced here: 386 us
  local copies, waits for them, and re-layouts  329 us (85%)
  waiting for transfers between devices  25.6 us (7%)
  matrix products  15.7 us (4%)
  between operations  13.5 us (3%)
    gather x2, local copies, waits for them, and re-layouts, labels(): occ_part = jnp.take(occ_irrep, index // nvir)  197 us
    gather x2, local copies, waits for them, and re-layouts, labels(): vir_part = jnp.take(vir_irrep, index % nvir)  132 us
    reduce_scatter x1, waiting for transfers between devices, body(): lax.psum_scatter(lax.dot_general(gathered, masked, dims, preferred_elemen...  24.8 us
    dot_general x1, matrix products, body(): lax.dot_general(gathered, masked, dims, preferred_element_type=jnp.float32)  15.7 us
  transfers between devices with their start and end apart: 2, of which 1 were waited for; matrix products, arithmetic and copies ran while one was open for 86% of the time, Pallas kernels for 0%

commit v1 on v0

v1 whole, which is shorter than its diff:
```python
import functools

import jax
import jax.numpy as jnp
from jax import lax
from jax.experimental import pallas as pl
from jax.experimental.pallas import tpu as pltpu
from jax.sharding import PartitionSpec as P
from math import gcd

MESH = pl.DeviceIdType.MESH
NT = (((1,), (1,)), ((), ()))


def kernel(nrow, ncol, kc, occ_ref, vir_row, vir_col, w_hbm, a_hbm, out_ref,
           gath, wm, acc, red, w_sem, own_sem, send_sem, recv_sem, rs_send, rs_recv):
    rho = lax.axis_index("row")
    kap = lax.axis_index("col")
    chips = nrow // 2
    chip = rho // 2
    core = rho % 2
    other = chip * 2 + 1 - core
    rows, depth = a_hbm.shape
    nr = w_hbm.shape[0]
    nvir = vir_row.shape[1]
    nq = depth // kc
    per_q = kc // nvir
    spo = nrow // ncol
    sub = gcd(nr, nvir)
    has_up = chip < chips - 1
    has_down = chip > 0

    def w_copy(j):
        cols = pl.ds(pl.multiple_of(j * nvir, nvir), nvir)
        return pltpu.make_async_copy(w_hbm.at[:, cols], wm.at[:, cols], w_sem.at[j])

    def chunk(q):
        return pl.ds(pl.multiple_of(q * kc, kc), kc)

    def own_copy(q):
        return pltpu.make_async_copy(a_hbm.at[:, chunk(q)], gath.at[rho, :, chunk(q)], own_sem.at[q])

    def remote(way, s, q, own=False):
        target = (rho + 2, rho - 2, other)[way]
        src = a_hbm.at[:, chunk(q)] if own else gath.at[s, :, chunk(q)]
        return pltpu.make_async_remote_copy(
            src_ref=src, dst_ref=gath.at[s, :, chunk(q)],
            send_sem=send_sem.at[way, s, q], recv_sem=recv_sem.at[s, q],
            device_id=(target, kap), device_id_type=MESH)

    def reduce_copy(s):
        return pltpu.make_async_remote_copy(
            src_ref=acc.at[s], dst_ref=red.at[kap, s % spo],
            send_sem=rs_send.at[s], recv_sem=rs_recv.at[kap, s % spo],
            device_id=(rho, s // spo), device_id_type=MESH)

    def loop(n, f):
        def step(i, c):
            f(i)
            return c
        lax.fori_loop(0, n, step, 0)

    loop(nq, lambda q: own_copy(q).start())
    loop(nq * per_q, lambda j: w_copy(j).start())

    barrier = pltpu.get_barrier_semaphore()

    @pl.when(has_up)
    def _():
        pl.semaphore_signal(barrier, inc=1, device_id=(rho + 2, kap), device_id_type=MESH)

    @pl.when(has_down)
    def _():
        pl.semaphore_signal(barrier, inc=1, device_id=(rho - 2, kap), device_id_type=MESH)

    pl.semaphore_signal(barrier, inc=1, device_id=(other, kap), device_id_type=MESH)
    for t in range(1, ncol):
        pl.semaphore_signal(barrier, inc=1, device_id=(rho, lax.rem(kap + t, ncol)), device_id_type=MESH)
    pl.semaphore_wait(barrier, ncol + has_up.astype(jnp.int32) + has_down.astype(jnp.int32))

    def send_own(q):
        @pl.when(has_up)
        def _():
            remote(0, rho, q, True).start()

        @pl.when(has_down)
        def _():
            remote(1, rho, q, True).start()

        remote(2, rho, q, True).start()

    loop(nq, send_own)
    acc[...] = jnp.zeros_like(acc)

    def mask(j):
        w_copy(j).wait()
        cols = pl.ds(pl.multiple_of(j * nvir, nvir), nvir)
        col_labels = vir_row[...] ^ occ_ref[kap * (depth // nvir) + j]
        for b in range(nr // sub):
            start = rho * nr + b * sub
            at = pl.multiple_of(lax.rem(start, nvir), sub)
            row_labels = vir_col[pl.ds(at, sub), :] ^ occ_ref[start // nvir]
            block = wm[b * sub:(b + 1) * sub, cols].astype(jnp.float32)
            kept = jnp.where(row_labels == col_labels, block, 0.0)
            wm[b * sub:(b + 1) * sub, cols] = kept.astype(wm.dtype)

    def product(p, q):
        a = gath[pl.ds(2 * p, 2), :, chunk(q)].reshape(2 * rows, kc)
        part = lax.dot_general(a, wm[:, chunk(q)], NT, preferred_element_type=jnp.float32)
        acc[pl.ds(2 * p, 2)] += part.reshape(2, rows, nr)

    def finish(p):
        for e in range(2):
            s = 2 * p + e

            @pl.when(s // spo != kap)
            def _():
                reduce_copy(s).start()

    def own_step(q):
        loop(per_q, lambda j: mask(q * per_q + j))
        own_copy(q).wait()
        remote(2, other, q).wait_recv()
        product(chip, q)

    loop(nq, own_step)
    finish(chip)

    def far_step(i):
        d = i // nq + 1
        q = i % nq
        for way in range(2):
            p = chip - d if way == 0 else chip + d
            there = p >= 0 if way == 0 else p < chips
            onward = has_up if way == 0 else has_down

            @pl.when(there)
            def _():
                s = 2 * p + core
                remote(way, s, q).wait_recv()

                @pl.when(onward)
                def _():
                    remote(way, s, q).start()

                remote(2, s, q).start()

        for way in range(2):
            p = chip - d if way == 0 else chip + d
            there = p >= 0 if way == 0 else p < chips

            @pl.when(there)
            def _():
                remote(2, 2 * p + 1 - core, q).wait_recv()
                product(p, q)

                @pl.when(q == nq - 1)
                def _():
                    finish(p)

    loop((chips - 1) * nq, far_step)

    for i in range(spo):
        total = acc[kap * spo + i]
        for t in range(1, ncol):
            peer = lax.rem(kap + t, ncol)
            pltpu.make_async_remote_copy(
                src_ref=acc.at[i], dst_ref=red.at[peer, i],
                send_sem=rs_send.at[i], recv_sem=rs_recv.at[peer, i],
                device_id=(rho, peer), device_id_type=MESH).wait_recv()
            total = total + red[peer, i]
        out_ref[i * rows:(i + 1) * rows, :] = total

    def drain(i):
        p = i // nq
        q = i % nq
        s = 2 * p + core

        @pl.when(has_up & (p <= chip))
        def _():
            remote(0, s, q).wait_send()

        @pl.when(has_down & (p >= chip))
        def _():
            remote(1, s, q).wait_send()

        remote(2, s, q).wait_send()

    loop(chips * nq, drain)

    def drain_reduce(s):
        @pl.when(s // spo != kap)
        def _():
            reduce_copy(s).wait_send()

    loop(nrow, drain_reduce)


def body(nrow, ncol, occ_irrep, vir_irrep, w_slab, amplitudes):
    rows, depth = amplitudes.shape
    nr = w_slab.shape[0]
    nvir = vir_irrep.shape[0]
    kc = 4096 if depth % 4096 == 0 else depth
    nq = depth // kc
    spo = nrow // ncol
    vmem = pl.BlockSpec(memory_space=pltpu.VMEM)
    anywhere = pl.BlockSpec(memory_space=pl.ANY)
    return pl.pallas_call(
        functools.partial(kernel, nrow, ncol, kc),
        out_shape=jax.ShapeDtypeStruct((spo * rows, nr), jnp.float32),
        in_specs=[pl.BlockSpec(memory_space=pltpu.SMEM), vmem, vmem, anywhere, anywhere],
        out_specs=vmem,
        scratch_shapes=[
            pltpu.VMEM((nrow, rows, depth), amplitudes.dtype),
            pltpu.VMEM((nr, depth), w_slab.dtype),
            pltpu.VMEM((nrow, rows, nr), jnp.float32),
            pltpu.VMEM((ncol, spo, rows, nr), jnp.float32),
            pltpu.SemaphoreType.DMA((depth // nvir,)),
            pltpu.SemaphoreType.DMA((nq,)),
            pltpu.SemaphoreType.DMA((3, nrow, nq)),
            pltpu.SemaphoreType.DMA((nrow, nq)),
            pltpu.SemaphoreType.DMA((nrow,)),
            pltpu.SemaphoreType.DMA((ncol, spo)),
        ],
        compiler_params=pltpu.CompilerParams(
            collective_id=0, has_side_effects=True, vmem_limit_bytes=56 * 1024 * 1024),
        cost_estimate=pl.CostEstimate(
            flops=2 * nrow * rows * nr * depth, bytes_accessed=2 * nr * depth, transcendentals=0),
    )(occ_irrep, vir_irrep.reshape(1, nvir), vir_irrep.reshape(nvir, 1), w_slab, amplitudes)


def solution(mesh):
    placed = (P(), P(), P("row", "col"), P("row", "col"))
    shape = dict(mesh.shape)
    return jax.shard_map(
        functools.partial(body, shape["row"], shape["col"]), mesh=mesh,
        in_specs=placed, out_specs=P("col", "row"), check_vma=False)
```

time: 388 us -> 155 us (0.40)
  local copies, waits for them, and re-layouts: 329 us -> 3.24 us
  Pallas kernels: 0 us -> 151 us
  waiting for transfers between devices: 25.6 us -> 0 us
  matrix products: 15.7 us -> 0 us
  between operations: 13.5 us -> 0.01 us
    gather x4 -> x0, local copies, waits for them, and re-layouts: 328 us -> none  [the longest x2 197 us: labels(): occ_part = jnp.take(occ_irrep, index // nvir)]
    pallas_call x0 -> x1, Pallas kernels: none -> 151 us  [body(): pl.pallas_call(functools.partial(kernel, nrow, ncol, kc), out_shape=jax.S...]
    reduce_scatter x1 -> x0, waiting for transfers between devices: 24.8 us -> none  [body(): lax.psum_scatter(lax.dot_general(gathered, masked, dims, preferred_elemen...]
    dot_general x1 -> x0, matrix products: 15.7 us -> none  [body(): lax.dot_general(gathered, masked, dims, preferred_element_type=jnp.float32)]
  transfers between devices with their start and end apart: 2 -> 0, of which waited for: 1 -> 0; matrix products, arithmetic and copies ran while one was open for 86% -> 0% of each run, Pallas kernels for 0% -> 0%
where the time goes in v1:
time: 155 us; the launch traced here: 154 us
  Pallas kernels  151 us (97%)
  local copies, waits for them, and re-layouts  3.24 us (2%)
    pallas_call x1, Pallas kernels, body(): pl.pallas_call(functools.partial(kernel, nrow, ncol, kc), out_shape=jax.S...  151 us

profile of v1, /device:TPU:6, one launch (start us, length us, event | category | flops | bytes accessed | tf_op | source)
XLA Modules:
  0.0 154.0 jit_solution(13759054584001346462)
XLA Ops:
  0.0 1.7 %copy.5.vir_col = s32[1024,1]{1,0:T(8,128)} copy(s32[1024,1]{0,1:T(1,128)} %bitcast.2) | data formatting | bytes 8192 | tf_op jit(solution)/shard_map/reshape | solution.py:229
  1.7 150.7 %shard_map.46 = f32[64,384]{1,0:T(8,128)} custom-call(s32[128]{0:T(128)} %occ_ref.1, s32[1,1024]{1,0:T(1,128)} %bitcast.3, s32[1024,1]{1,0:T(8,128)} %copy.5.vir_col, bf16[384,32768]{1,0:T(8,128)(2,1)} %w_hbm.1, bf16[32,32768]{1,0:T(8,128)(2,1)} %a_hbm.1), custom_call_target="tpu_custom_call" | custom-call | flops 6442450944 | bytes 25165824 | tf_op jit(solution)/shard_map/pallas_call | solution.py:208
  152.4 1.5 %copy.7 = f32[64,384]{1,0:T(8,128)} copy(f32[64,384]{1,0:T(8,128)} %shard_map.46) | data formatting | bytes 196608

commit v2 on v1

--- a/solution.py
+++ b/solution.py
@@ -10,10 +10,13 @@
 
 MESH = pl.DeviceIdType.MESH
 NT = (((1,), (1,)), ((), ()))
-
-
-def kernel(nrow, ncol, kc, occ_ref, vir_row, vir_col, w_hbm, a_hbm, out_ref,
-           gath, wm, acc, red, w_sem, own_sem, send_sem, recv_sem, rs_send, rs_recv):
+KC = 2048
+
+
+def kernel(nrow, ncol, kc, nh, cap, occ_ref, vir_row, w_hbm, a_hbm, out_ref,
+           gath, wm, acc, red, row_lab, w_sem, own_sem, send_sem, recv_sem, rs_send, rs_recv,
+           v_out=None, v_in=None, w_help=None, p_out=None, p_in=None, help_lab=None,
+           spread=None, fold=None, v_send=None, v_recv=None, p_send=None, p_recv=None):
     rho = lax.axis_index("row")
     kap = lax.axis_index("col")
     chips = nrow // 2
@@ -29,6 +32,19 @@
     sub = gcd(nr, nvir)
     has_up = chip < chips - 1
     has_down = chip > 0
+    if nh:
+        first, last = chip == 0, chip == chips - 1
+        is_end = first | last
+        below, above = chip == 1, chip == chips - 2
+        helper = below | above
+        up_from = jnp.where(above, nh, 0)
+        down_from = jnp.where(below, nh, 0)
+        lead = nq - 2 * nh
+        helped = jnp.where(below, rho - 2, rho + 2)
+        end_chip = jnp.where(below, 0, chips - 1)
+        patron = jnp.where(first, rho + 2, rho - 2)
+    else:
+        up_from = down_from = 0
 
     def w_copy(j):
         cols = pl.ds(pl.multiple_of(j * nvir, nvir), nvir)
@@ -78,31 +94,134 @@
         pl.semaphore_signal(barrier, inc=1, device_id=(rho, lax.rem(kap + t, ncol)), device_id_type=MESH)
     pl.semaphore_wait(barrier, ncol + has_up.astype(jnp.int32) + has_down.astype(jnp.int32))
 
+    def send_far(q):
+        @pl.when(has_up & (q >= up_from))
+        def _():
+            remote(0, rho, q, True).start()
+
+        @pl.when(has_down & (q >= down_from))
+        def _():
+            remote(1, rho, q, True).start()
+
     def send_own(q):
-        @pl.when(has_up)
-        def _():
-            remote(0, rho, q, True).start()
-
-        @pl.when(has_down)
-        def _():
-            remote(1, rho, q, True).start()
-
         remote(2, rho, q, True).start()
+        if nh:
+            @pl.when((q < lead) | jnp.logical_not(is_end))
+            def _():
+                send_far(q)
+        else:
+            send_far(q)
 
     loop(nq, send_own)
     acc[...] = jnp.zeros_like(acc)
+
+    def lane_labels(owner, b):
+        start = owner * nr + b * sub
+        at = pl.multiple_of(lax.rem(start, nvir), sub)
+        return (vir_row[:, pl.ds(at, sub)] ^ occ_ref[start // nvir]).astype(jnp.float32)
+
+    sub_i = lax.broadcasted_iota(jnp.int32, (sub, sub), 0)
+    lane_i = lax.broadcasted_iota(jnp.int32, (sub, sub), 1)
+
+    def write_labels(owner, ref):
+        for b in range(nr // sub):
+            wide = jnp.broadcast_to(lane_labels(owner, b), (sub, sub))
+            ref[b * sub:(b + 1) * sub, :] = jnp.sum(
+                jnp.where(sub_i == lane_i, wide, 0.0), axis=1, keepdims=True)
+
+    def col_labels(j):
+        return (vir_row[...] ^ occ_ref[kap * (depth // nvir) + j]).astype(jnp.float32)
+
+    write_labels(rho, row_lab)
 
     def mask(j):
         w_copy(j).wait()
         cols = pl.ds(pl.multiple_of(j * nvir, nvir), nvir)
-        col_labels = vir_row[...] ^ occ_ref[kap * (depth // nvir) + j]
+        labels = col_labels(j)
         for b in range(nr // sub):
-            start = rho * nr + b * sub
-            at = pl.multiple_of(lax.rem(start, nvir), sub)
-            row_labels = vir_col[pl.ds(at, sub), :] ^ occ_ref[start // nvir]
             block = wm[b * sub:(b + 1) * sub, cols].astype(jnp.float32)
-            kept = jnp.where(row_labels == col_labels, block, 0.0)
+            kept = jnp.where(row_lab[b * sub:(b + 1) * sub, :] == labels, block, 0.0)
             wm[b * sub:(b + 1) * sub, cols] = kept.astype(wm.dtype)
+
+    if nh:
+        def v_copy(g):
+            return pltpu.make_async_remote_copy(
+                src_ref=v_out.at[g], dst_ref=v_in.at[g],
+                send_sem=v_send.at[g], recv_sem=v_recv.at[g],
+                device_id=(patron, kap), device_id_type=MESH)
+
+        def p_copy(p):
+            at = pl.ds(2 * p, 2)
+            return pltpu.make_async_remote_copy(
+                src_ref=p_out.at[at], dst_ref=p_in.at[at],
+                send_sem=p_send.at[p], recv_sem=p_recv.at[p],
+                device_id=(helped, kap), device_id_type=MESH)
+
+        @pl.when(is_end)
+        def _():
+            for b in range(nr // sub):
+                mine = lane_labels(rho, b)
+                rank = jnp.zeros((1, sub), jnp.float32)
+                for c in range(b + 1):
+                    same = row_lab[c * sub:(c + 1) * sub, :] == mine
+                    if c == b:
+                        same = same & (sub_i < lane_i)
+                    rank = rank + jnp.sum(jnp.where(same, 1.0, 0.0), axis=0, keepdims=True)
+                slot = lax.broadcasted_iota(jnp.int32, (cap, sub), 0).astype(jnp.float32)
+                fold[:, b * sub:(b + 1) * sub] = jnp.where(slot == rank, 1.0, 0.0).astype(fold.dtype)
+
+        @pl.when(helper)
+        def _():
+            p_out[...] = jnp.zeros_like(p_out)
+            write_labels(helped, help_lab)
+            for b in range(nr // sub):
+                mine = help_lab[b * sub:(b + 1) * sub, :]
+                rank = jnp.zeros((sub, 1), jnp.float32)
+                for c in range(b + 1):
+                    same = mine == lane_labels(helped, c)
+                    if c == b:
+                        same = same & (lane_i < sub_i)
+                    rank = rank + jnp.sum(jnp.where(same, 1.0, 0.0), axis=1, keepdims=True)
+                slot = lax.broadcasted_iota(jnp.int32, (sub, cap), 1).astype(jnp.float32)
+                spread[b * sub:(b + 1) * sub, :] = jnp.where(slot == rank, 1.0, 0.0).astype(spread.dtype)
+
+        def send_folded(g):
+            def part(j):
+                at = pl.ds(pl.multiple_of(j * nvir, nvir), nvir)
+                cols = pl.ds(pl.multiple_of(g * kc + j * nvir, nvir), nvir)
+                v = jnp.dot(fold[...], wm[:, cols], preferred_element_type=jnp.float32)
+                v_out[g, :, at] = v.astype(v_out.dtype)
+
+            loop(per_q, part)
+            v_copy(g).start()
+            send_far(lead + 2 * g)
+            send_far(lead + 2 * g + 1)
+
+        def help_with(g):
+            v_copy(g).wait_recv()
+
+            def part(j):
+                at = pl.ds(pl.multiple_of(j * nvir, nvir), nvir)
+                labels = col_labels(g * per_q + j)
+                for b in range(nr // sub):
+                    rows_b = slice(b * sub, (b + 1) * sub)
+                    block = jnp.dot(spread[rows_b, :], v_in[g, :, at], preferred_element_type=jnp.float32)
+                    kept = jnp.where(help_lab[rows_b, :] == labels, block, 0.0)
+                    w_help[rows_b, at] = kept.astype(w_help.dtype)
+
+            loop(per_q, part)
+
+            def one(t):
+                p = jnp.where(below, t + 1, t)
+                a = gath[pl.ds(2 * p, 2), :, chunk(g)].reshape(2 * rows, kc)
+                p_part = lax.dot_general(a, w_help[...], NT, preferred_element_type=jnp.float32)
+                p_out[pl.ds(2 * p, 2)] += p_part.reshape(2, rows, nr)
+
+                @pl.when(g == nh - 1)
+                def _():
+                    p_copy(p).start()
+
+            loop(chips - 1, one)
 
     def product(p, q):
         a = gath[pl.ds(2 * p, 2), :, chunk(q)].reshape(2 * rows, kc)
@@ -119,6 +238,11 @@
 
     def own_step(q):
         loop(per_q, lambda j: mask(q * per_q + j))
+        if nh:
+            @pl.when(is_end & (q < nh))
+            def _():
+                send_folded(q)
+
         own_copy(q).wait()
         remote(2, other, q).wait_recv()
         product(chip, q)
@@ -126,13 +250,29 @@
     loop(nq, own_step)
     finish(chip)
 
-    def far_step(i):
+    def source(way, i):
         d = i // nq + 1
         q = i % nq
+        p = chip - d if way == 0 else chip + d
+        there = p >= 0 if way == 0 else p < chips
+        if nh:
+            there = there & jnp.logical_not(is_end & (q < nh))
+            slow = below if way == 0 else above
+            j = jnp.maximum(i - lead + 2, 0)
+            g = (2 * j + 1) // 9
+            off = j - (9 * g) // 2
+            early = i < lead
+            later = (i >= lead) & (g >= 1) & (g <= nh) & (off >= 1) & (off <= 2)
+            slow_q = jnp.where(early, i, jnp.where(later, lead + 2 * (g - 1) + off - 1, 0))
+            p = jnp.where(slow, end_chip, p)
+            q = jnp.where(slow, slow_q, q)
+            there = (slow & (early | later)) | (jnp.logical_not(slow) & there)
+        return p, q, there
+
+    def far_step(i):
         for way in range(2):
-            p = chip - d if way == 0 else chip + d
-            there = p >= 0 if way == 0 else p < chips
-            onward = has_up if way == 0 else has_down
+            p, q, there = source(way, i)
+            onward = has_up & (q >= up_from) if way == 0 else has_down & (q >= down_from)
 
             @pl.when(there)
             def _():
@@ -146,19 +286,45 @@
                 remote(2, s, q).start()
 
         for way in range(2):
-            p = chip - d if way == 0 else chip + d
-            there = p >= 0 if way == 0 else p < chips
+            p, q, there = source(way, i)
 
             @pl.when(there)
             def _():
                 remote(2, 2 * p + 1 - core, q).wait_recv()
                 product(p, q)
 
-                @pl.when(q == nq - 1)
+                @pl.when((q == nq - 1) & jnp.logical_not(is_end) if nh else q == nq - 1)
                 def _():
                     finish(p)
 
+        if nh:
+            def maybe(g):
+                ready = jnp.maximum(lead - 2 + (9 * (g + 1)) // 2, (chips - 3) * nq + g)
+
+                @pl.when(i == ready)
+                def _():
+                    help_with(g)
+
+            @pl.when(helper)
+            def _():
+                loop(nh, maybe)
+
     loop((chips - 1) * nq, far_step)
+
+    if nh:
+        @pl.when(is_end)
+        def _():
+            def settle(t):
+                p = jnp.where(first, t + 1, chips - 2 - t)
+                at = pl.ds(2 * p, 2)
+                pltpu.make_async_remote_copy(
+                    src_ref=p_out.at[at], dst_ref=p_in.at[at],
+                    send_sem=p_send.at[p], recv_sem=p_recv.at[p],
+                    device_id=(patron, kap), device_id_type=MESH).wait_recv()
+                acc[at] += p_in[at]
+                finish(p)
+
+            loop(chips - 1, settle)
 
     for i in range(spo):
         total = acc[kap * spo + i]
@@ -176,17 +342,28 @@
         q = i % nq
         s = 2 * p + core
 
-        @pl.when(has_up & (p <= chip))
+        @pl.when(has_up & (p <= chip) & (q >= up_from))
         def _():
             remote(0, s, q).wait_send()
 
-        @pl.when(has_down & (p >= chip))
+        @pl.when(has_down & (p >= chip) & (q >= down_from))
         def _():
             remote(1, s, q).wait_send()
 
-        remote(2, s, q).wait_send()
+        @pl.when((p == chip) | jnp.logical_not(is_end & (q < nh)) if nh else p >= 0)
+        def _():
+            remote(2, s, q).wait_send()
 
     loop(chips * nq, drain)
+
+    if nh:
+        @pl.when(is_end)
+        def _():
+            loop(nh, lambda g: v_copy(g).wait_send())
+
+        @pl.when(helper)
+        def _():
+            loop(chips - 1, lambda t: p_copy(jnp.where(below, t + 1, t)).wait_send())
 
     def drain_reduce(s):
         @pl.when(s // spo != kap)
@@ -200,33 +377,63 @@
     rows, depth = amplitudes.shape
     nr = w_slab.shape[0]
     nvir = vir_irrep.shape[0]
-    kc = 4096 if depth % 4096 == 0 else depth
+    kc = KC if depth % KC == 0 else depth
     nq = depth // kc
     spo = nrow // ncol
+    cap = -(-nr * 5 // 24 // 16) * 16
+    help_chunks = 3 * nq // 8 if nrow // 2 >= 4 else 0
     vmem = pl.BlockSpec(memory_space=pltpu.VMEM)
     anywhere = pl.BlockSpec(memory_space=pl.ANY)
-    return pl.pallas_call(
-        functools.partial(kernel, nrow, ncol, kc),
-        out_shape=jax.ShapeDtypeStruct((spo * rows, nr), jnp.float32),
-        in_specs=[pl.BlockSpec(memory_space=pltpu.SMEM), vmem, vmem, anywhere, anywhere],
-        out_specs=vmem,
-        scratch_shapes=[
+
+    def call(nh, *args):
+        scratch = [
             pltpu.VMEM((nrow, rows, depth), amplitudes.dtype),
             pltpu.VMEM((nr, depth), w_slab.dtype),
             pltpu.VMEM((nrow, rows, nr), jnp.float32),
             pltpu.VMEM((ncol, spo, rows, nr), jnp.float32),
+            pltpu.VMEM((nr, 1), jnp.float32),
             pltpu.SemaphoreType.DMA((depth // nvir,)),
             pltpu.SemaphoreType.DMA((nq,)),
             pltpu.SemaphoreType.DMA((3, nrow, nq)),
             pltpu.SemaphoreType.DMA((nrow, nq)),
             pltpu.SemaphoreType.DMA((nrow,)),
             pltpu.SemaphoreType.DMA((ncol, spo)),
-        ],
-        compiler_params=pltpu.CompilerParams(
-            collective_id=0, has_side_effects=True, vmem_limit_bytes=56 * 1024 * 1024),
-        cost_estimate=pl.CostEstimate(
-            flops=2 * nrow * rows * nr * depth, bytes_accessed=2 * nr * depth, transcendentals=0),
-    )(occ_irrep, vir_irrep.reshape(1, nvir), vir_irrep.reshape(nvir, 1), w_slab, amplitudes)
+        ]
+        if nh:
+            scratch += [
+                pltpu.VMEM((nh, cap, kc), w_slab.dtype),
+                pltpu.VMEM((nh, cap, kc), w_slab.dtype),
+                pltpu.VMEM((nr, kc), w_slab.dtype),
+                pltpu.VMEM((nrow, rows, nr), jnp.float32),
+                pltpu.VMEM((nrow, rows, nr), jnp.float32),
+                pltpu.VMEM((nr, 1), jnp.float32),
+                pltpu.VMEM((nr, cap), w_slab.dtype),
+                pltpu.VMEM((cap, nr), w_slab.dtype),
+                pltpu.SemaphoreType.DMA((nh,)),
+                pltpu.SemaphoreType.DMA((nh,)),
+                pltpu.SemaphoreType.DMA((nrow // 2,)),
+                pltpu.SemaphoreType.DMA((nrow // 2,)),
+            ]
+        return pl.pallas_call(
+            functools.partial(kernel, nrow, ncol, kc, nh, cap),
+            out_shape=jax.ShapeDtypeStruct((spo * rows, nr), jnp.float32),
+            in_specs=[pl.BlockSpec(memory_space=pltpu.SMEM), vmem, anywhere, anywhere],
+            out_specs=vmem,
+            scratch_shapes=scratch,
+            compiler_params=pltpu.CompilerParams(
+                collective_id=1 if nh else 0, has_side_effects=True, vmem_limit_bytes=58 * 1024 * 1024),
+            cost_estimate=pl.CostEstimate(
+                flops=2 * nrow * rows * nr * depth, bytes_accessed=2 * nr * depth, transcendentals=0),
+        )(*args)
+
+    args = (occ_irrep, vir_irrep.reshape(1, nvir), w_slab, amplitudes)
+    if not help_chunks:
+        return call(0, *args)
+    nocc = -(-nrow * nr // nvir)
+    labels = (occ_irrep[:nocc, None] ^ vir_irrep[None, :]).reshape(-1)[:nrow * nr].reshape(nrow, 1, nr)
+    counts = jnp.sum(labels == jnp.arange(8, dtype=jnp.int32).reshape(1, 8, 1), axis=2)
+    fits = jnp.max(counts) <= cap
+    return lax.cond(fits, functools.partial(call, help_chunks), functools.partial(call, 0), *args)
 
 
 def solution(mesh):

time: 155 us -> 145 us (0.935)
  Pallas kernels: 151 us -> 141 us
  local copies, waits for them, and re-layouts: 3.24 us -> 0.66 us
  other arithmetic: 0 us -> 1.61 us
    pallas_call x1, Pallas kernels: 151 us -> 141 us  [call(): pl.pallas_call(functools.partial(kernel, nrow, ncol, kc, nh, cap), out_sh...]
    reshape x1 -> x0, local copies, waits for them, and re-layouts: 1.7 us -> none  [body(): vir_irrep.reshape(nvir, 1)]
where the time goes in v2:
time: 145 us; the launch traced here: 144 us
  Pallas kernels  141 us (97%)
  other arithmetic  1.61 us (1%)
    pallas_call x1, Pallas kernels, call(): pl.pallas_call(functools.partial(kernel, nrow, ncol, kc, nh, cap), out_sh...  141 us

profile of v2, /device:TPU:6, one launch (start us, length us, event | category | flops | bytes accessed | tf_op | source)
XLA Modules:
  0.0 144.3 jit_solution(12727665379022400286)
XLA Ops:
  0.0 0.8 broadcast_xor_fusion
  0.8 0.2 convert_reduce_fusion
  1.0 0.6 reduce_max.9
  2.3 141.3 %conditional.1 = (f32[64,384]{1,0:T(8,128)S(1)}) conditional(s32[]{:T(128)} %convert_element_type.7, (s32[128]{0:T(128)}, s32[1024]{0:T(1024)}, bf16[384,32768]{1,0:T(8,128)(2,1)}, bf16[32,32768]{1,0:T(8,128)(2,1)}) %tuple.11, (s32[128]{0:T(128)}, s32[1024]{0:T(1024)}, bf16[384,32768]{1,0:T(8,128)(2,1)}, bf16[32,32768]{1,0:T(8,128)(2,1)}) %tuple.11), branch_computations={%region_2.0_spmd, %region_3.0_spmd} | conditional | flops 6442450944 | bytes 25165832 | solution.py:436
  2.3 141.3 %branch_1_fun.1 = f32[64,384]{1,0:T(8,128)S(1)} custom-call(s32[128]{0:T(128)} %get-tuple-element.28.occ_ref, s32[1,1024]{1,0:T(1,128)} %bitcast.4, bf16[384,32768]{1,0:T(8,128)(2,1)} %get-tuple-element.40.w_hbm, bf16[32,32768]{1,0:T(8,128)(2,1)} %get-tuple-element.42.a_hbm), custom_call_target="tpu_custom_call" | custom-call | flops 6442450944 | bytes 25165824 | tf_op jit(solution)/shard_map/cond/branch_1_fun/pallas_call | solution.py:417
  143.6 0.6 copy.14
  (1 shorter events, 0.0 us)

commit v3 on v2

--- a/solution.py
+++ b/solution.py
@@ -14,8 +14,8 @@
 
 
 def kernel(nrow, ncol, kc, nh, cap, occ_ref, vir_row, w_hbm, a_hbm, out_ref,
-           gath, wm, acc, red, row_lab, w_sem, own_sem, send_sem, recv_sem, rs_send, rs_recv,
-           v_out=None, v_in=None, w_help=None, p_out=None, p_in=None, help_lab=None,
+           gath, wm, acc, done, red, row_lab, w_sem, own_sem, send_sem, recv_sem, rs_send, rs_recv,
+           v_out=None, v_in=None, w_help=None, p_acc=None, p_out=None, p_in=None, help_lab=None,
            spread=None, fold=None, v_send=None, v_recv=None, p_send=None, p_recv=None):
     rho = lax.axis_index("row")
     kap = lax.axis_index("col")
@@ -66,7 +66,7 @@
 
     def reduce_copy(s):
         return pltpu.make_async_remote_copy(
-            src_ref=acc.at[s], dst_ref=red.at[kap, s % spo],
+            src_ref=done.at[s], dst_ref=red.at[kap, s % spo],
             send_sem=rs_send.at[s], recv_sem=rs_recv.at[kap, s % spo],
             device_id=(rho, s // spo), device_id_type=MESH)
 
@@ -172,7 +172,7 @@
 
         @pl.when(helper)
         def _():
-            p_out[...] = jnp.zeros_like(p_out)
+            p_acc[...] = jnp.zeros_like(p_acc)
             write_labels(helped, help_lab)
             for b in range(nr // sub):
                 mine = help_lab[b * sub:(b + 1) * sub, :]
@@ -214,21 +214,22 @@
             def one(t):
                 p = jnp.where(below, t + 1, t)
                 a = gath[pl.ds(2 * p, 2), :, chunk(g)].reshape(2 * rows, kc)
-                p_part = lax.dot_general(a, w_help[...], NT, preferred_element_type=jnp.float32)
-                p_out[pl.ds(2 * p, 2)] += p_part.reshape(2, rows, nr)
+                p_acc[p] += lax.dot_general(w_help[...], a, NT, preferred_element_type=jnp.float32)
 
                 @pl.when(g == nh - 1)
                 def _():
+                    p_out[pl.ds(2 * p, 2)] = p_acc[p].T.reshape(2, rows, nr)
                     p_copy(p).start()
 
             loop(chips - 1, one)
 
     def product(p, q):
         a = gath[pl.ds(2 * p, 2), :, chunk(q)].reshape(2 * rows, kc)
-        part = lax.dot_general(a, wm[:, chunk(q)], NT, preferred_element_type=jnp.float32)
-        acc[pl.ds(2 * p, 2)] += part.reshape(2, rows, nr)
-
-    def finish(p):
+        acc[p] += lax.dot_general(wm[:, chunk(q)], a, NT, preferred_element_type=jnp.float32)
+
+    def finish(p, more=None):
+        whole = acc[p].T.reshape(2, rows, nr)
+        done[pl.ds(2 * p, 2)] = whole if more is None else whole + more[pl.ds(2 * p, 2)]
         for e in range(2):
             s = 2 * p + e
 
@@ -321,17 +322,16 @@
                     src_ref=p_out.at[at], dst_ref=p_in.at[at],
                     send_sem=p_send.at[p], recv_sem=p_recv.at[p],
                     device_id=(patron, kap), device_id_type=MESH).wait_recv()
-                acc[at] += p_in[at]
-                finish(p)
+                finish(p, p_in)
 
             loop(chips - 1, settle)
 
     for i in range(spo):
-        total = acc[kap * spo + i]
+        total = done[kap * spo + i]
         for t in range(1, ncol):
             peer = lax.rem(kap + t, ncol)
             pltpu.make_async_remote_copy(
-                src_ref=acc.at[i], dst_ref=red.at[peer, i],
+                src_ref=done.at[i], dst_ref=red.at[peer, i],
                 send_sem=rs_send.at[i], recv_sem=rs_recv.at[peer, i],
                 device_id=(rho, peer), device_id_type=MESH).wait_recv()
             total = total + red[peer, i]
@@ -389,6 +389,7 @@
         scratch = [
             pltpu.VMEM((nrow, rows, depth), amplitudes.dtype),
             pltpu.VMEM((nr, depth), w_slab.dtype),
+            pltpu.VMEM((nrow // 2, nr, 2 * rows), jnp.float32),
             pltpu.VMEM((nrow, rows, nr), jnp.float32),
             pltpu.VMEM((ncol, spo, rows, nr), jnp.float32),
             pltpu.VMEM((nr, 1), jnp.float32),
@@ -404,6 +405,7 @@
                 pltpu.VMEM((nh, cap, kc), w_slab.dtype),
                 pltpu.VMEM((nh, cap, kc), w_slab.dtype),
                 pltpu.VMEM((nr, kc), w_slab.dtype),
+                pltpu.VMEM((nrow // 2, nr, 2 * rows), jnp.float32),
                 pltpu.VMEM((nrow, rows, nr), jnp.float32),
                 pltpu.VMEM((nrow, rows, nr), jnp.float32),
                 pltpu.VMEM((nr, 1), jnp.float32),

time: 145 us -> 142 us (0.979)
  Pallas kernels: 141 us -> 138 us
    pallas_call x1, Pallas kernels: 141 us -> 138 us  [call(): pl.pallas_call(functools.partial(kernel, nrow, ncol, kc, nh, cap), out_sh...]
where the time goes in v3:
time: 142 us; the launch traced here: 141 us
  Pallas kernels  138 us (97%)
  other arithmetic  1.61 us (1%)
    pallas_call x1, Pallas kernels, call(): pl.pallas_call(functools.partial(kernel, nrow, ncol, kc, nh, cap), out_sh...  138 us

profile of v3, /device:TPU:6, one launch (start us, length us, event | category | flops | bytes accessed | tf_op | source)
XLA Modules:
  0.0 140.8 jit_solution(6614058074228057823)
XLA Ops:
  0.0 0.8 broadcast_xor_fusion
  0.8 0.2 convert_reduce_fusion
  1.0 0.6 reduce_max.9
  2.3 137.8 %conditional.1 = (f32[64,384]{1,0:T(8,128)S(1)}) conditional(s32[]{:T(128)} %convert_element_type.7, (s32[128]{0:T(128)}, s32[1024]{0:T(1024)}, bf16[384,32768]{1,0:T(8,128)(2,1)}, bf16[32,32768]{1,0:T(8,128)(2,1)}) %tuple.11, (s32[128]{0:T(128)}, s32[1024]{0:T(1024)}, bf16[384,32768]{1,0:T(8,128)(2,1)}, bf16[32,32768]{1,0:T(8,128)(2,1)}) %tuple.11), branch_computations={%region_2.0_spmd, %region_3.0_spmd} | conditional | flops 6442450944 | bytes 25165832 | solution.py:438
  2.3 137.8 %branch_1_fun.1 = f32[64,384]{1,0:T(8,128)S(1)} custom-call(s32[128]{0:T(128)} %get-tuple-element.28.occ_ref, s32[1,1024]{1,0:T(1,128)} %bitcast.4, bf16[384,32768]{1,0:T(8,128)(2,1)} %get-tuple-element.40.w_hbm, bf16[32,32768]{1,0:T(8,128)(2,1)} %get-tuple-element.42.a_hbm), custom_call_target="tpu_custom_call" | custom-call | flops 6442450944 | bytes 25165824 | tf_op jit(solution)/shard_map/cond/branch_1_fun/pallas_call | solution.py:419
  140.1 0.6 copy.14
  (1 shorter events, 0.0 us)

commit v4 on v3

--- a/solution.py
+++ b/solution.py
@@ -11,6 +11,7 @@
 MESH = pl.DeviceIdType.MESH
 NT = (((1,), (1,)), ((), ()))
 KC = 2048
+AHEAD = 5
 
 
 def kernel(nrow, ncol, kc, nh, cap, occ_ref, vir_row, w_hbm, a_hbm, out_ref,
@@ -39,9 +40,7 @@
         helper = below | above
         up_from = jnp.where(above, nh, 0)
         down_from = jnp.where(below, nh, 0)
-        lead = nq - 2 * nh
         helped = jnp.where(below, rho - 2, rho + 2)
-        end_chip = jnp.where(below, 0, chips - 1)
         patron = jnp.where(first, rho + 2, rho - 2)
     else:
         up_from = down_from = 0
@@ -94,25 +93,35 @@
         pl.semaphore_signal(barrier, inc=1, device_id=(rho, lax.rem(kap + t, ncol)), device_id_type=MESH)
     pl.semaphore_wait(barrier, ncol + has_up.astype(jnp.int32) + has_down.astype(jnp.int32))
 
-    def send_far(q):
-        @pl.when(has_up & (q >= up_from))
-        def _():
-            remote(0, rho, q, True).start()
-
-        @pl.when(has_down & (q >= down_from))
-        def _():
-            remote(1, rho, q, True).start()
-
-    def send_own(q):
-        remote(2, rho, q, True).start()
-        if nh:
-            @pl.when((q < lead) | jnp.logical_not(is_end))
-            def _():
-                send_far(q)
-        else:
-            send_far(q)
-
-    loop(nq, send_own)
+    ahead = min(AHEAD, nq)
+
+    def counted(n, skip):
+        return (n // nq) * (nq - skip) + jnp.maximum(n % nq - skip, 0)
+
+    def sendable(way, n):
+        skip = up_from if way == 0 else down_from
+        reach = chip + 1 if way == 0 else chips - chip
+        seen = counted(n, jnp.where(is_end, nh, 0)) if nh else n
+        most = jnp.minimum(nq - skip + counted(n, skip), (nq - skip) * reach)
+        most = jnp.minimum(most, ahead + seen)
+        return jnp.where(has_up if way == 0 else has_down, most, 0)
+
+    def send_between(way, lo, hi):
+        skip = up_from if way == 0 else down_from
+
+        def send(m, c):
+            d = lax.div(m, nq - skip)
+            q = skip + lax.rem(m, nq - skip)
+            p = chip - d if way == 0 else chip + d
+            remote(way, 2 * p + core, q).start()
+            return c
+
+        lax.fori_loop(lo, hi, send, 0)
+
+    loop(nq, lambda q: own_copy(q).wait())
+    for way in range(2):
+        send_between(way, 0, sendable(way, 0))
+    loop(nq, lambda q: remote(2, rho, q, True).start())
     acc[...] = jnp.zeros_like(acc)
 
     def lane_labels(owner, b):
@@ -185,7 +194,7 @@
                 slot = lax.broadcasted_iota(jnp.int32, (sub, cap), 1).astype(jnp.float32)
                 spread[b * sub:(b + 1) * sub, :] = jnp.where(slot == rank, 1.0, 0.0).astype(spread.dtype)
 
-        def send_folded(g):
+        def make_folded(g):
             def part(j):
                 at = pl.ds(pl.multiple_of(j * nvir, nvir), nvir)
                 cols = pl.ds(pl.multiple_of(g * kc + j * nvir, nvir), nvir)
@@ -193,9 +202,11 @@
                 v_out[g, :, at] = v.astype(v_out.dtype)
 
             loop(per_q, part)
-            v_copy(g).start()
-            send_far(lead + 2 * g)
-            send_far(lead + 2 * g + 1)
+
+        def v_ready(n):
+            seen = counted(n, nh) - (nq - ahead + 2)
+            ready = jnp.clip((seen + 2) // 2, 0, nh)
+            return jnp.where(n <= nq, 0, jnp.where(n == (chips - 1) * nq, nh, ready))
 
         def help_with(g):
             v_copy(g).wait_recv()
@@ -242,14 +253,14 @@
         if nh:
             @pl.when(is_end & (q < nh))
             def _():
-                send_folded(q)
-
-        own_copy(q).wait()
+                make_folded(q)
+
         remote(2, other, q).wait_recv()
         product(chip, q)
 
-    loop(nq, own_step)
-    finish(chip)
+        @pl.when(q == nq - 1)
+        def _():
+            finish(chip)
 
     def source(way, i):
         d = i // nq + 1
@@ -258,33 +269,33 @@
         there = p >= 0 if way == 0 else p < chips
         if nh:
             there = there & jnp.logical_not(is_end & (q < nh))
-            slow = below if way == 0 else above
-            j = jnp.maximum(i - lead + 2, 0)
-            g = (2 * j + 1) // 9
-            off = j - (9 * g) // 2
-            early = i < lead
-            later = (i >= lead) & (g >= 1) & (g <= nh) & (off >= 1) & (off <= 2)
-            slow_q = jnp.where(early, i, jnp.where(later, lead + 2 * (g - 1) + off - 1, 0))
-            p = jnp.where(slow, end_chip, p)
-            q = jnp.where(slow, slow_q, q)
-            there = (slow & (early | later)) | (jnp.logical_not(slow) & there)
         return p, q, there
 
-    def far_step(i):
+    def step(i):
+        @pl.when(i < nq)
+        def _():
+            own_step(i)
+
         for way in range(2):
             p, q, there = source(way, i)
-            onward = has_up & (q >= up_from) if way == 0 else has_down & (q >= down_from)
 
             @pl.when(there)
             def _():
                 s = 2 * p + core
                 remote(way, s, q).wait_recv()
-
-                @pl.when(onward)
-                def _():
-                    remote(way, s, q).start()
-
                 remote(2, s, q).start()
+
+        for way in range(2):
+            send_between(way, sendable(way, i), sendable(way, i + 1))
+
+        if nh:
+            @pl.when(is_end)
+            def _():
+                def send_v(g, c):
+                    v_copy(g).start()
+                    return c
+
+                lax.fori_loop(v_ready(i), v_ready(i + 1), send_v, 0)
 
         for way in range(2):
             p, q, there = source(way, i)
@@ -300,7 +311,7 @@
 
         if nh:
             def maybe(g):
-                ready = jnp.maximum(lead - 2 + (9 * (g + 1)) // 2, (chips - 3) * nq + g)
+                ready = (chips - 3) * nq + (nq * (g + 1)) // nh - 1
 
                 @pl.when(i == ready)
                 def _():
@@ -310,7 +321,7 @@
             def _():
                 loop(nh, maybe)
 
-    loop((chips - 1) * nq, far_step)
+    loop((chips - 1) * nq, step)
 
     if nh:
         @pl.when(is_end)

time: 142 us -> 131 us (0.923); the launches traced: 141 us -> 131 us
  Pallas kernels: 138 us -> 128 us
    pallas_call x1, Pallas kernels: 138 us -> 128 us  [call(): pl.pallas_call(functools.partial(kernel, nrow, ncol, kc, nh, cap), out_sh...]
where the time goes in v4:
time: 131 us
  Pallas kernels  128 us (98%)
  other arithmetic  1.61 us (1%)
    pallas_call x1, Pallas kernels, call(): pl.pallas_call(functools.partial(kernel, nrow, ncol, kc, nh, cap), out_sh...  128 us

profile of v4, /device:TPU:6, one launch (start us, length us, event | category | flops | bytes accessed | tf_op | source)
XLA Modules:
  0.0 131.2 jit_solution(5171065961236998033)
XLA Ops:
  0.0 0.8 broadcast_xor_fusion
  0.8 0.2 convert_reduce_fusion
  1.0 0.6 reduce_max.9
  2.3 128.3 %conditional.1 = (f32[64,384]{1,0:T(8,128)S(1)}) conditional(s32[]{:T(128)} %convert_element_type.7, (s32[128]{0:T(128)}, s32[1024]{0:T(1024)}, bf16[384,32768]{1,0:T(8,128)(2,1)}, bf16[32,32768]{1,0:T(8,128)(2,1)}) %tuple.11, (s32[128]{0:T(128)}, s32[1024]{0:T(1024)}, bf16[384,32768]{1,0:T(8,128)(2,1)}, bf16[32,32768]{1,0:T(8,128)(2,1)}) %tuple.11), branch_computations={%region_2.0_spmd, %region_3.0_spmd} | conditional | flops 6442450944 | bytes 25165832 | solution.py:449
  2.3 128.3 %branch_1_fun.1 = f32[64,384]{1,0:T(8,128)S(1)} custom-call(s32[128]{0:T(128)} %get-tuple-element.28.occ_ref, s32[1,1024]{1,0:T(1,128)} %bitcast.4, bf16[384,32768]{1,0:T(8,128)(2,1)} %get-tuple-element.40.w_hbm, bf16[32,32768]{1,0:T(8,128)(2,1)} %get-tuple-element.42.a_hbm), custom_call_target="tpu_custom_call" | custom-call | flops 6442450944 | bytes 25165824 | tf_op jit(solution)/shard_map/cond/branch_1_fun/pallas_call | solution.py:430
  130.6 0.6 copy.14
  (1 shorter events, 0.0 us)

commit v5 on v4

--- a/solution.py
+++ b/solution.py
@@ -15,8 +15,8 @@
 
 
 def kernel(nrow, ncol, kc, nh, cap, occ_ref, vir_row, w_hbm, a_hbm, out_ref,
-           gath, wm, acc, done, red, row_lab, w_sem, own_sem, send_sem, recv_sem, rs_send, rs_recv,
-           v_out=None, v_in=None, w_help=None, p_acc=None, p_out=None, p_in=None, help_lab=None,
+           gath, wm, acc, near, done, red, row_lab, row_key, w_sem, own_sem, send_sem, recv_sem, rs_send, rs_recv,
+           v_out=None, v_in=None, w_help=None, p_acc=None, p_out=None, p_in=None, help_lab=None, help_key=None,
            spread=None, fold=None, v_send=None, v_recv=None, p_send=None, p_recv=None):
     rho = lax.axis_index("row")
     kap = lax.axis_index("col")
@@ -123,6 +123,7 @@
         send_between(way, 0, sendable(way, 0))
     loop(nq, lambda q: remote(2, rho, q, True).start())
     acc[...] = jnp.zeros_like(acc)
+    near[...] = jnp.zeros_like(near)
 
     def lane_labels(owner, b):
         start = owner * nr + b * sub
@@ -132,25 +133,29 @@
     sub_i = lax.broadcasted_iota(jnp.int32, (sub, sub), 0)
     lane_i = lax.broadcasted_iota(jnp.int32, (sub, sub), 1)
 
-    def write_labels(owner, ref):
+    def write_labels(owner, ref, key):
         for b in range(nr // sub):
             wide = jnp.broadcast_to(lane_labels(owner, b), (sub, sub))
             ref[b * sub:(b + 1) * sub, :] = jnp.sum(
                 jnp.where(sub_i == lane_i, wide, 0.0), axis=1, keepdims=True)
+        key[...] = jnp.broadcast_to(ref[...], key.shape).astype(key.dtype)
 
     def col_labels(j):
-        return (vir_row[...] ^ occ_ref[kap * (depth // nvir) + j]).astype(jnp.float32)
-
-    write_labels(rho, row_lab)
+        return (vir_row[...] ^ occ_ref[kap * (depth // nvir) + j]).astype(jnp.float32).astype(wm.dtype)
+
+    write_labels(rho, row_lab, row_key)
+
+    def keep(key, labels, block):
+        key = jnp.concatenate([key] * (nvir // key.shape[1]), axis=1)
+        return jnp.where(key == labels, block, jnp.zeros_like(block))
 
     def mask(j):
         w_copy(j).wait()
         cols = pl.ds(pl.multiple_of(j * nvir, nvir), nvir)
         labels = col_labels(j)
         for b in range(nr // sub):
-            block = wm[b * sub:(b + 1) * sub, cols].astype(jnp.float32)
-            kept = jnp.where(row_lab[b * sub:(b + 1) * sub, :] == labels, block, 0.0)
-            wm[b * sub:(b + 1) * sub, cols] = kept.astype(wm.dtype)
+            block = wm[b * sub:(b + 1) * sub, cols]
+            wm[b * sub:(b + 1) * sub, cols] = keep(row_key[b * sub:(b + 1) * sub, :], labels, block)
 
     if nh:
         def v_copy(g):
@@ -182,7 +187,7 @@
         @pl.when(helper)
         def _():
             p_acc[...] = jnp.zeros_like(p_acc)
-            write_labels(helped, help_lab)
+            write_labels(helped, help_lab, help_key)
             for b in range(nr // sub):
                 mine = help_lab[b * sub:(b + 1) * sub, :]
                 rank = jnp.zeros((sub, 1), jnp.float32)
@@ -217,22 +222,18 @@
                 for b in range(nr // sub):
                     rows_b = slice(b * sub, (b + 1) * sub)
                     block = jnp.dot(spread[rows_b, :], v_in[g, :, at], preferred_element_type=jnp.float32)
-                    kept = jnp.where(help_lab[rows_b, :] == labels, block, 0.0)
-                    w_help[rows_b, at] = kept.astype(w_help.dtype)
+                    w_help[rows_b, at] = keep(help_key[rows_b, :], labels, block.astype(w_help.dtype))
 
             loop(per_q, part)
 
-            def one(t):
-                p = jnp.where(below, t + 1, t)
-                a = gath[pl.ds(2 * p, 2), :, chunk(g)].reshape(2 * rows, kc)
-                p_acc[p] += lax.dot_general(w_help[...], a, NT, preferred_element_type=jnp.float32)
-
-                @pl.when(g == nh - 1)
-                def _():
-                    p_out[pl.ds(2 * p, 2)] = p_acc[p].T.reshape(2, rows, nr)
-                    p_copy(p).start()
-
-            loop(chips - 1, one)
+            base = jnp.where(below, 2, 0)
+            a = gath[pl.ds(base, nrow - 2), :, chunk(g)].reshape((nrow - 2) * rows, kc)
+            p_acc[...] += lax.dot_general(w_help[...], a, NT, preferred_element_type=jnp.float32)
+
+            @pl.when(g == nh - 1)
+            def _():
+                p_out[pl.ds(base, nrow - 2)] = p_acc[...].T.reshape(nrow - 2, rows, nr)
+                loop(chips - 1, lambda t: p_copy(jnp.where(below, t + 1, t)).start())
 
     def product(p, q):
         a = gath[pl.ds(2 * p, 2), :, chunk(q)].reshape(2 * rows, kc)
@@ -241,12 +242,27 @@
     def finish(p, more=None):
         whole = acc[p].T.reshape(2, rows, nr)
         done[pl.ds(2 * p, 2)] = whole if more is None else whole + more[pl.ds(2 * p, 2)]
+        send_done(p)
+
+    def send_done(p):
         for e in range(2):
             s = 2 * p + e
 
             @pl.when(s // spo != kap)
             def _():
                 reduce_copy(s).start()
+
+    inner = has_up & has_down
+
+    def product_near(q):
+        base = 2 * (chip - 1)
+        a = gath[pl.ds(base, 6), :, chunk(q)].reshape(6 * rows, kc)
+        near[...] += lax.dot_general(wm[:, chunk(q)], a, NT, preferred_element_type=jnp.float32)
+
+        @pl.when(q == nq - 1)
+        def _():
+            done[pl.ds(base, 6)] = near[...].T.reshape(6, rows, nr)
+            loop(3, lambda t: send_done(chip - 1 + t))
 
     def own_step(q):
         loop(per_q, lambda j: mask(q * per_q + j))
@@ -256,11 +272,14 @@
                 make_folded(q)
 
         remote(2, other, q).wait_recv()
-        product(chip, q)
-
-        @pl.when(q == nq - 1)
-        def _():
-            finish(chip)
+
+        @pl.when(jnp.logical_not(inner))
+        def _():
+            product(chip, q)
+
+            @pl.when(q == nq - 1)
+            def _():
+                finish(chip)
 
     def source(way, i):
         d = i // nq + 1
@@ -303,11 +322,18 @@
             @pl.when(there)
             def _():
                 remote(2, 2 * p + 1 - core, q).wait_recv()
-                product(p, q)
-
-                @pl.when((q == nq - 1) & jnp.logical_not(is_end) if nh else q == nq - 1)
+
+                @pl.when(jnp.logical_not(inner & (i < nq)))
                 def _():
-                    finish(p)
+                    product(p, q)
+
+                    @pl.when((q == nq - 1) & jnp.logical_not(is_end) if nh else q == nq - 1)
+                    def _():
+                        finish(p)
+
+        @pl.when(inner & (i < nq))
+        def _():
+            product_near(i)
 
         if nh:
             def maybe(g):
@@ -401,9 +427,11 @@
             pltpu.VMEM((nrow, rows, depth), amplitudes.dtype),
             pltpu.VMEM((nr, depth), w_slab.dtype),
             pltpu.VMEM((nrow // 2, nr, 2 * rows), jnp.float32),
+            pltpu.VMEM((nr, 6 * rows), jnp.float32),
             pltpu.VMEM((nrow, rows, nr), jnp.float32),
             pltpu.VMEM((ncol, spo, rows, nr), jnp.float32),
             pltpu.VMEM((nr, 1), jnp.float32),
+            pltpu.VMEM((nr, 128), w_slab.dtype),
             pltpu.SemaphoreType.DMA((depth // nvir,)),
             pltpu.SemaphoreType.DMA((nq,)),
             pltpu.SemaphoreType.DMA((3, nrow, nq)),
@@ -416,10 +444,11 @@
                 pltpu.VMEM((nh, cap, kc), w_slab.dtype),
                 pltpu.VMEM((nh, cap, kc), w_slab.dtype),
                 pltpu.VMEM((nr, kc), w_slab.dtype),
-                pltpu.VMEM((nrow // 2, nr, 2 * rows), jnp.float32),
+                pltpu.VMEM((nr, (nrow - 2) * rows), jnp.float32),
                 pltpu.VMEM((nrow, rows, nr), jnp.float32),
                 pltpu.VMEM((nrow, rows, nr), jnp.float32),
                 pltpu.VMEM((nr, 1), jnp.float32),
+                pltpu.VMEM((nr, 128), w_slab.dtype),
                 pltpu.VMEM((nr, cap), w_slab.dtype),
                 pltpu.VMEM((cap, nr), w_slab.dtype),
                 pltpu.SemaphoreType.DMA((nh,)),

time: 131 us -> 124 us (0.947)
  Pallas kernels: 128 us -> 121 us
    pallas_call x1, Pallas kernels: 128 us -> 121 us  [call(): pl.pallas_call(functools.partial(kernel, nrow, ncol, kc, nh, cap), out_sh...]
where the time goes in v5:
time: 124 us
  Pallas kernels  121 us (98%)
  other arithmetic  1.61 us (1%)
    pallas_call x1, Pallas kernels, call(): pl.pallas_call(functools.partial(kernel, nrow, ncol, kc, nh, cap), out_sh...  121 us

profile of v5, /device:TPU:6, one launch (start us, length us, event | category | flops | bytes accessed | tf_op | source)
XLA Modules:
  0.0 123.9 jit_solution(1006898450603815509)
XLA Ops:
  0.0 0.8 broadcast_xor_fusion
  0.8 0.2 convert_reduce_fusion
  1.0 0.6 reduce_max.9
  2.3 121.0 %conditional.1 = (f32[64,384]{1,0:T(8,128)S(1)}) conditional(s32[]{:T(128)} %convert_element_type.7, (s32[128]{0:T(128)}, s32[1024]{0:T(1024)}, bf16[384,32768]{1,0:T(8,128)(2,1)}, bf16[32,32768]{1,0:T(8,128)(2,1)}) %tuple.11, (s32[128]{0:T(128)}, s32[1024]{0:T(1024)}, bf16[384,32768]{1,0:T(8,128)(2,1)}, bf16[32,32768]{1,0:T(8,128)(2,1)}) %tuple.11), branch_computations={%region_2.0_spmd, %region_3.0_spmd} | conditional | flops 6442450944 | bytes 25165832 | solution.py:478
  2.3 120.9 %branch_1_fun.1 = f32[64,384]{1,0:T(8,128)S(1)} custom-call(s32[128]{0:T(128)} %get-tuple-element.28.occ_ref, s32[1,1024]{1,0:T(1,128)} %bitcast.4, bf16[384,32768]{1,0:T(8,128)(2,1)} %get-tuple-element.40.w_hbm, bf16[32,32768]{1,0:T(8,128)(2,1)} %get-tuple-element.42.a_hbm), custom_call_target="tpu_custom_call" | custom-call | flops 6442450944 | bytes 25165824 | tf_op jit(solution)/shard_map/cond/branch_1_fun/pallas_call | solution.py:459
  123.3 0.6 copy.14
  (1 shorter events, 0.0 us)

commit v6 on v5

--- a/solution.py
+++ b/solution.py
@@ -98,12 +98,23 @@
     def counted(n, skip):
         return (n // nq) * (nq - skip) + jnp.maximum(n % nq - skip, 0)
 
+    def slow(x):
+        tail = nq // 4
+        lead = nq - nh - tail
+        between = jnp.clip((2 * (x - lead)) // 7, 0, nh)
+        return jnp.minimum(x, lead) + between + jnp.clip(x - lead - (7 * nh) // 2, 0, tail)
+
     def sendable(way, n):
         skip = up_from if way == 0 else down_from
         reach = chip + 1 if way == 0 else chips - chip
-        seen = counted(n, jnp.where(is_end, nh, 0)) if nh else n
-        most = jnp.minimum(nq - skip + counted(n, skip), (nq - skip) * reach)
-        most = jnp.minimum(most, ahead + seen)
+        passed = counted(n, skip)
+        if nh:
+            passed = jnp.where(below if way == 0 else above, slow(n), passed)
+        most = jnp.minimum(nq - skip + passed, (nq - skip) * reach)
+        limit = ahead + n
+        if nh:
+            limit = jnp.where(is_end, slow(ahead + 2 + counted(n, nh)), limit)
+        most = jnp.minimum(most, limit)
         return jnp.where(has_up if way == 0 else has_down, most, 0)
 
     def send_between(way, lo, hi):
@@ -209,9 +220,8 @@
             loop(per_q, part)
 
         def v_ready(n):
-            seen = counted(n, nh) - (nq - ahead + 2)
-            ready = jnp.clip((seen + 2) // 2, 0, nh)
-            return jnp.where(n <= nq, 0, jnp.where(n == (chips - 1) * nq, nh, ready))
+            x = ahead + 2 + counted(n, nh) - (nq - nh - nq // 4)
+            return jnp.clip((2 * x + 2) // 7, 0, nh)
 
         def help_with(g):
             v_copy(g).wait_recv()
@@ -255,14 +265,15 @@
     inner = has_up & has_down
 
     def product_near(q):
-        base = 2 * (chip - 1)
-        a = gath[pl.ds(base, 6), :, chunk(q)].reshape(6 * rows, kc)
+        wide = nrow if nh else 6
+        base = 0 if nh else 2 * (chip - 1)
+        a = gath[pl.ds(base, wide), :, chunk(q)].reshape(wide * rows, kc)
         near[...] += lax.dot_general(wm[:, chunk(q)], a, NT, preferred_element_type=jnp.float32)
 
         @pl.when(q == nq - 1)
         def _():
-            done[pl.ds(base, 6)] = near[...].T.reshape(6, rows, nr)
-            loop(3, lambda t: send_done(chip - 1 + t))
+            done[pl.ds(base, wide)] = near[...].T.reshape(wide, rows, nr)
+            loop(wide // 2, lambda t: send_done(base // 2 + t))
 
     def own_step(q):
         loop(per_q, lambda j: mask(q * per_q + j))
@@ -288,12 +299,34 @@
         there = p >= 0 if way == 0 else p < chips
         if nh:
             there = there & jnp.logical_not(is_end & (q < nh))
+            there = there & jnp.logical_not(below if way == 0 else above)
         return p, q, there
+
+    def settle(t):
+        p = jnp.where(first, t + 1, chips - 2 - t)
+        at = pl.ds(2 * p, 2)
+        pltpu.make_async_remote_copy(
+            src_ref=p_out.at[at], dst_ref=p_in.at[at],
+            send_sem=p_send.at[p], recv_sem=p_recv.at[p],
+            device_id=(patron, kap), device_id_type=MESH).wait_recv()
+        finish(p, p_in)
+
+    def slow_loop(i, f):
+        def one(q, c):
+            f(jnp.where(below, core, nrow - 2 + core), q)
+            return c
+
+        lax.fori_loop(jnp.where(helper, slow(i), 0), jnp.where(helper, slow(i + 1), 0), one, 0)
 
     def step(i):
         @pl.when(i < nq)
         def _():
             own_step(i)
+
+        if nh:
+            @pl.when(is_end & (i == (chips - 1) * nq - 1))
+            def _():
+                loop(chips - 2, settle)
 
         for way in range(2):
             p, q, there = source(way, i)
@@ -304,6 +337,13 @@
                 remote(way, s, q).wait_recv()
                 remote(2, s, q).start()
 
+        if nh:
+            def take(s, q):
+                remote(0, s, q).wait_recv()
+                remote(2, s, q).start()
+
+            slow_loop(i, take)
+
         for way in range(2):
             send_between(way, sendable(way, i), sendable(way, i + 1))
 
@@ -323,7 +363,7 @@
             def _():
                 remote(2, 2 * p + 1 - core, q).wait_recv()
 
-                @pl.when(jnp.logical_not(inner & (i < nq)))
+                @pl.when(is_end if nh else jnp.logical_not(inner & (i < nq)))
                 def _():
                     product(p, q)
 
@@ -331,13 +371,20 @@
                     def _():
                         finish(p)
 
-        @pl.when(inner & (i < nq))
-        def _():
-            product_near(i)
+        if nh:
+            slow_loop(i, lambda s, q: remote(2, s + 1 - 2 * core, q).wait_recv())
+
+            @pl.when(inner & (i >= nq) & (i < 2 * nq))
+            def _():
+                product_near(i - nq)
+        else:
+            @pl.when(inner & (i < nq))
+            def _():
+                product_near(i)
 
         if nh:
             def maybe(g):
-                ready = (chips - 3) * nq + (nq * (g + 1)) // nh - 1
+                ready = jnp.maximum(nq + g + 1, (2 * (nq - nh - nq // 4) + 7 * g + 6) // 2 - 1)
 
                 @pl.when(i == ready)
                 def _():
@@ -352,16 +399,7 @@
     if nh:
         @pl.when(is_end)
         def _():
-            def settle(t):
-                p = jnp.where(first, t + 1, chips - 2 - t)
-                at = pl.ds(2 * p, 2)
-                pltpu.make_async_remote_copy(
-                    src_ref=p_out.at[at], dst_ref=p_in.at[at],
-                    send_sem=p_send.at[p], recv_sem=p_recv.at[p],
-                    device_id=(patron, kap), device_id_type=MESH).wait_recv()
-                finish(p, p_in)
-
-            loop(chips - 1, settle)
+            settle(chips - 2)
 
     for i in range(spo):
         total = done[kap * spo + i]
@@ -418,7 +456,7 @@
     nq = depth // kc
     spo = nrow // ncol
     cap = -(-nr * 5 // 24 // 16) * 16
-    help_chunks = 3 * nq // 8 if nrow // 2 >= 4 else 0
+    help_chunks = 3 * nq // 8 if nrow // 2 == 4 else 0
     vmem = pl.BlockSpec(memory_space=pltpu.VMEM)
     anywhere = pl.BlockSpec(memory_space=pl.ANY)
 
@@ -427,7 +465,7 @@
             pltpu.VMEM((nrow, rows, depth), amplitudes.dtype),
             pltpu.VMEM((nr, depth), w_slab.dtype),
             pltpu.VMEM((nrow // 2, nr, 2 * rows), jnp.float32),
-            pltpu.VMEM((nr, 6 * rows), jnp.float32),
+            pltpu.VMEM((nr, (nrow if nh else 6) * rows), jnp.float32),
             pltpu.VMEM((nrow, rows, nr), jnp.float32),
             pltpu.VMEM((ncol, spo, rows, nr), jnp.float32),
             pltpu.VMEM((nr, 1), jnp.float32),

time: 124 us -> 126 us (1.016)
  Pallas kernels: 121 us -> 123 us
    pallas_call x1, Pallas kernels: 121 us -> 123 us  [call(): pl.pallas_call(functools.partial(kernel, nrow, ncol, kc, nh, cap), out_sh...]
where the time goes in v6:
time: 126 us
  Pallas kernels  123 us (98%)
  other arithmetic  1.61 us (1%)
    pallas_call x1, Pallas kernels, call(): pl.pallas_call(functools.partial(kernel, nrow, ncol, kc, nh, cap), out_sh...  123 us

profile of v6, /device:TPU:6, one launch (start us, length us, event | category | flops | bytes accessed | tf_op | source)
XLA Modules:
  0.0 125.9 jit_solution(12150218328326559189)
XLA Ops:
  0.0 0.8 broadcast_xor_fusion
  0.8 0.2 convert_reduce_fusion
  1.0 0.6 reduce_max.9
  2.3 122.9 %conditional.1 = (f32[64,384]{1,0:T(8,128)S(1)}) conditional(s32[]{:T(128)} %convert_element_type.7, (s32[128]{0:T(128)}, s32[1024]{0:T(1024)}, bf16[384,32768]{1,0:T(8,128)(2,1)}, bf16[32,32768]{1,0:T(8,128)(2,1)}) %tuple.11, (s32[128]{0:T(128)}, s32[1024]{0:T(1024)}, bf16[384,32768]{1,0:T(8,128)(2,1)}, bf16[32,32768]{1,0:T(8,128)(2,1)}) %tuple.11), branch_computations={%region_2.0_spmd, %region_3.0_spmd} | conditional | flops 6442450944 | bytes 25165832 | solution.py:516
  2.3 122.9 %branch_1_fun.1 = f32[64,384]{1,0:T(8,128)S(1)} custom-call(s32[128]{0:T(128)} %get-tuple-element.28.occ_ref, s32[1,1024]{1,0:T(1,128)} %bitcast.4, bf16[384,32768]{1,0:T(8,128)(2,1)} %get-tuple-element.40.w_hbm, bf16[32,32768]{1,0:T(8,128)(2,1)} %get-tuple-element.42.a_hbm), custom_call_target="tpu_custom_call" | custom-call | flops 6442450944 | bytes 25165824 | tf_op jit(solution)/shard_map/cond/branch_1_fun/pallas_call | solution.py:497
  125.2 0.6 copy.14
  (1 shorter events, 0.0 us)

commit v7 on v5

--- a/solution.py
+++ b/solution.py
@@ -290,10 +290,24 @@
             there = there & jnp.logical_not(is_end & (q < nh))
         return p, q, there
 
+    def settle(t):
+        p = jnp.where(first, t + 1, chips - 2 - t)
+        at = pl.ds(2 * p, 2)
+        pltpu.make_async_remote_copy(
+            src_ref=p_out.at[at], dst_ref=p_in.at[at],
+            send_sem=p_send.at[p], recv_sem=p_recv.at[p],
+            device_id=(patron, kap), device_id_type=MESH).wait_recv()
+        finish(p, p_in)
+
     def step(i):
         @pl.when(i < nq)
         def _():
             own_step(i)
+
+        if nh:
+            @pl.when(is_end & (i == (chips - 1) * nq - 1))
+            def _():
+                loop(chips - 2, settle)
 
         for way in range(2):
             p, q, there = source(way, i)
@@ -337,7 +351,7 @@
 
         if nh:
             def maybe(g):
-                ready = (chips - 3) * nq + (nq * (g + 1)) // nh - 1
+                ready = (chips - 3) * nq + (5 * (g + 1) + 1) // 2 - 1
 
                 @pl.when(i == ready)
                 def _():
@@ -352,16 +366,7 @@
     if nh:
         @pl.when(is_end)
         def _():
-            def settle(t):
-                p = jnp.where(first, t + 1, chips - 2 - t)
-                at = pl.ds(2 * p, 2)
-                pltpu.make_async_remote_copy(
-                    src_ref=p_out.at[at], dst_ref=p_in.at[at],
-                    send_sem=p_send.at[p], recv_sem=p_recv.at[p],
-                    device_id=(patron, kap), device_id_type=MESH).wait_recv()
-                finish(p, p_in)
-
-            loop(chips - 1, settle)
+            settle(chips - 2)
 
     for i in range(spo):
         total = done[kap * spo + i]
@@ -418,7 +423,7 @@
     nq = depth // kc
     spo = nrow // ncol
     cap = -(-nr * 5 // 24 // 16) * 16
-    help_chunks = 3 * nq // 8 if nrow // 2 >= 4 else 0
+    help_chunks = 5 * nq // 16 if nrow // 2 >= 4 else 0
     vmem = pl.BlockSpec(memory_space=pltpu.VMEM)
     anywhere = pl.BlockSpec(memory_space=pl.ANY)
 

time: 124 us -> 126 us (1.016)
  Pallas kernels: 121 us -> 123 us
    pallas_call x1, Pallas kernels: 121 us -> 123 us  [call(): pl.pallas_call(functools.partial(kernel, nrow, ncol, kc, nh, cap), out_sh...]
where the time goes in v7:
time: 126 us
  Pallas kernels  123 us (98%)
  other arithmetic  1.61 us (1%)
    pallas_call x1, Pallas kernels, call(): pl.pallas_call(functools.partial(kernel, nrow, ncol, kc, nh, cap), out_sh...  123 us

profile of v7, /device:TPU:6, one launch (start us, length us, event | category | flops | bytes accessed | tf_op | source)
XLA Modules:
  0.0 125.7 jit_solution(13911833403455160925)
XLA Ops:
  0.0 0.8 broadcast_xor_fusion
  0.8 0.2 convert_reduce_fusion
  1.0 0.6 reduce_max.9
  2.3 122.8 %conditional.1 = (f32[64,384]{1,0:T(8,128)S(1)}) conditional(s32[]{:T(128)} %convert_element_type.7, (s32[128]{0:T(128)}, s32[1024]{0:T(1024)}, bf16[384,32768]{1,0:T(8,128)(2,1)}, bf16[32,32768]{1,0:T(8,128)(2,1)}) %tuple.11, (s32[128]{0:T(128)}, s32[1024]{0:T(1024)}, bf16[384,32768]{1,0:T(8,128)(2,1)}, bf16[32,32768]{1,0:T(8,128)(2,1)}) %tuple.11), branch_computations={%region_2.0_spmd, %region_3.0_spmd} | conditional | flops 6442450944 | bytes 25165832 | solution.py:483
  2.3 122.8 %branch_1_fun.1 = f32[64,384]{1,0:T(8,128)S(1)} custom-call(s32[128]{0:T(128)} %get-tuple-element.28.occ_ref, s32[1,1024]{1,0:T(1,128)} %bitcast.4, bf16[384,32768]{1,0:T(8,128)(2,1)} %get-tuple-element.40.w_hbm, bf16[32,32768]{1,0:T(8,128)(2,1)} %get-tuple-element.42.a_hbm), custom_call_target="tpu_custom_call" | custom-call | flops 6442450944 | bytes 25165824 | tf_op jit(solution)/shard_map/cond/branch_1_fun/pallas_call | solution.py:464
  125.1 0.6 copy.14
  (1 shorter events, 0.0 us)
